TPU v7x, 32 devices: a whole 2x2x4 slice. The times are simulated.
32 devices in a mesh: seq: 8 (over y, x, core), dp: 4 (over z).
Axes of the slice: x: 2, y: 2, z: 4, core: 2. Of those that a mesh axis runs over, the one named last changes fastest.
Arguments:
- queries: bfloat16 [4, 1024, 4096], P('dp', 'seq'), may hold values from -6 to 6
- keys: bfloat16 [4, 1024, 512], P('dp', 'seq'), may hold values from -6 to 6
- values: bfloat16 [4, 1024, 512], P('dp', 'seq'), may hold values from -6 to 6
- attn_out: bfloat16 [4, 1024, 4096], P('dp', 'seq'), may hold values from -6 to 6
- out_grad: bfloat16 [4, 1024, 4096], P('dp', 'seq'), may hold values from -6 to 6
- segments: int32 [4, 1024], P('dp', 'seq'), may hold values from 0 to 7, never falling along the last dimension, each value on 1 to 256 neighbouring positions
- token_counts: int32 [4], P('dp'), may hold values from 341 to 1024
- head_slot: int32 [32], replicated, may hold values from 0 to 3, as said below
Outputs:
- query_grad: bfloat16 [4, 1024, 4096], P('dp', 'seq')
- key_grad: bfloat16 [4, 1024, 512], P('dp', 'seq')
- value_grad: bfloat16 [4, 1024, 512], P('dp', 'seq')
Inputs may be any that keep to these rules, and one draw needn't show every extreme that they name: `segments`: document ids of a packed sequence, never falling along it; a document holds at most 256 tokens. `head_slot`: never falling over the query heads; every KV head is read by at least one query head, groups may differ in size.
All inputs are finite; a program needn't handle non-finite values.
Results may differ from a plain program's by a relative error of at most 0.006.
Values may be sent and summed in bfloat16 or wider, within the bound.
A program may use at most 64 MiB of HBM per device.

v0:
```python
import math

import jax
import jax.numpy as jnp
from jax import lax
from jax.sharding import PartitionSpec as P

HEADS = 32
HEAD_DIM = 128
KV_SLOTS = 4


NEG_FILL = -1e30


def contract_rows(left, right):
    return lax.dot_general(
        left, right, (((1,), (1,)), ((), ())), preferred_element_type=jnp.float32
    )


def contract_cols(left, right):
    return lax.dot_general(
        left, right, (((0,), (0,)), ((), ())), preferred_element_type=jnp.float32
    )


def head_grads(query, key_rows, value_rows, grad_rows, row_delta, doc_ids):
    length, width = query.shape
    tile_rows = min(512, length)
    tile_count = length // tile_rows
    score_scale = 1.0 / math.sqrt(width)

    def rows_of(array, tile):
        return lax.dynamic_slice_in_dim(array, tile * tile_rows, tile_rows, 0)

    def tile_scores(query_tile, q_tile, k_tile):
        key_tile = rows_of(key_rows, k_tile)
        scores = contract_rows(query_tile, key_tile) * score_scale
        q_pos = q_tile * tile_rows + lax.broadcasted_iota(jnp.int32, (tile_rows, tile_rows), 0)
        k_pos = k_tile * tile_rows + lax.broadcasted_iota(jnp.int32, (tile_rows, tile_rows), 1)
        q_doc = rows_of(doc_ids, q_tile)
        k_doc = rows_of(doc_ids, k_tile)
        allowed = jnp.logical_and(k_pos <= q_pos, q_doc[:, None] == k_doc[None, :])
        return (key_tile, scores, allowed)

    def tile_live(q_tile, k_tile):
        first_query = lax.dynamic_index_in_dim(doc_ids, q_tile * tile_rows, 0, keepdims=False)
        last_key = lax.dynamic_index_in_dim(
            doc_ids, k_tile * tile_rows + tile_rows - 1, 0, keepdims=False
        )
        return jnp.logical_and(k_tile <= q_tile, last_key >= first_query)

    tiles = jnp.arange(tile_count, dtype=jnp.int32)

    def row_stats(q_tile):
        query_tile = rows_of(query, q_tile)

        def row_visit_tile(k_tile, running):

            def row_live_tile(tile_state):
                run_max, run_sum = tile_state
                _, scores, allowed = tile_scores(query_tile, q_tile, k_tile)
                scores = jnp.where(allowed, scores, NEG_FILL)
                new_max = jnp.maximum(run_max, jnp.max(scores, axis=1))
                probs = jnp.where(allowed, jnp.exp(scores - new_max[:, None]), 0.0)
                return (new_max, run_sum * jnp.exp(run_max - new_max) + jnp.sum(probs, axis=1))

            return lax.cond(
                tile_live(q_tile, k_tile), row_live_tile, lambda tile_state: tile_state, running
            )

        start_state = (
            jnp.full((tile_rows,), NEG_FILL, jnp.float32),
            jnp.zeros((tile_rows,), jnp.float32),
        )
        run_max, run_sum = lax.fori_loop(
            jnp.int32(0), jnp.int32(tile_count), row_visit_tile, start_state
        )
        return run_max + jnp.log(run_sum)

    log_sums = lax.map(row_stats, tiles)

    def query_pass(running, q_tile):
        key_total, value_total = running
        query_tile = rows_of(query, q_tile)
        grad_tile = rows_of(grad_rows, q_tile)
        delta_tile = rows_of(row_delta, q_tile)
        log_tile = lax.dynamic_index_in_dim(log_sums, q_tile, 0, keepdims=False)

        def query_visit_tile(k_tile, tile_state):

            def query_live_tile(inner):
                query_acc, key_acc, value_acc = inner
                key_tile, scores, allowed = tile_scores(query_tile, q_tile, k_tile)
                value_tile = rows_of(value_rows, k_tile)
                weights = jnp.where(allowed, jnp.exp(scores - log_tile[:, None]), 0.0)
                weights_half = weights.astype(jnp.bfloat16)
                value_add = contract_cols(weights_half, grad_tile)
                grad_weights = contract_rows(grad_tile, value_tile)
                score_grad = (weights * (grad_weights - delta_tile[:, None]) * score_scale).astype(
                    jnp.bfloat16
                )
                query_acc = query_acc + jnp.dot(
                    score_grad, key_tile, preferred_element_type=jnp.float32
                )
                key_add = contract_cols(score_grad, query_tile)
                start = k_tile * tile_rows
                key_acc = lax.dynamic_update_slice_in_dim(
                    key_acc, rows_of(key_acc, k_tile) + key_add, start, 0
                )
                value_acc = lax.dynamic_update_slice_in_dim(
                    value_acc, rows_of(value_acc, k_tile) + value_add, start, 0
                )
                return (query_acc, key_acc, value_acc)

            return lax.cond(
                tile_live(q_tile, k_tile), query_live_tile, lambda inner: inner, tile_state
            )

        start_state = (jnp.zeros((tile_rows, width), jnp.float32), key_total, value_total)
        query_acc, key_total, value_total = lax.fori_loop(
            jnp.int32(0), jnp.int32(tile_count), query_visit_tile, start_state
        )
        return ((key_total, value_total), query_acc)

    zero_rows = jnp.zeros((length, width), jnp.float32)
    (key_total, value_total), query_parts = lax.scan(query_pass, (zero_rows, zero_rows), tiles)
    return (query_parts.reshape(length, width), key_total, value_total)


def local(queries, keys, values, attn_out, out_grad, segments, token_counts, head_slot):
    group_size = lax.axis_size("seq")
    tok_rows = queries.shape[1]
    length = tok_rows * group_size
    heads_dev = HEADS // group_size
    own_width = heads_dev * HEAD_DIM
    token_total = lax.psum(jnp.sum(token_counts.astype(jnp.float32)), "dp")
    factor = lax.axis_size("dp") * length / token_total
    doc_ids = lax.all_gather(segments[0], "seq", axis=0, tiled=True)
    query_rows = queries[0]
    grad_rows = out_grad[0]
    query_own, grad_own, output_own = (
        lax.all_to_all(query_rows, "seq", split_axis=1, concat_axis=0, tiled=True),
        lax.all_to_all(grad_rows, "seq", split_axis=1, concat_axis=0, tiled=True),
        lax.all_to_all(attn_out[0], "seq", split_axis=1, concat_axis=0, tiled=True),
    )
    products = grad_own.astype(jnp.float32) * output_own.astype(jnp.float32)
    row_delta = jnp.sum(products.reshape(length, heads_dev, HEAD_DIM), axis=2)
    key_value = jnp.stack([keys[0], values[0]], axis=1).reshape(tok_rows, 2, KV_SLOTS, HEAD_DIM)
    gathered = lax.all_gather(key_value, "seq", axis=0, tiled=True)
    own_slots = lax.dynamic_slice_in_dim(head_slot, lax.axis_index("seq") * heads_dev, heads_dev)
    kv_own = jnp.take(gathered, own_slots, axis=2)
    query_heads = query_own.reshape(length, heads_dev, HEAD_DIM)
    grad_heads = grad_own.reshape(length, heads_dev, HEAD_DIM)
    key_heads = kv_own[:, 0]
    value_heads = kv_own[:, 1]

    def one_head(head_index):

        def select_head(array):
            return lax.dynamic_index_in_dim(array, head_index, 1, keepdims=False)

        query_part, key_part, value_part = head_grads(
            select_head(query_heads),
            select_head(key_heads),
            select_head(value_heads),
            select_head(grad_heads),
            select_head(row_delta),
            doc_ids,
        )
        return (
            (factor * query_part).astype(jnp.bfloat16),
            (factor * key_part).astype(jnp.bfloat16),
            (factor * value_part).astype(jnp.bfloat16),
        )

    query_parts, key_parts, value_parts = lax.map(one_head, jnp.arange(heads_dev, dtype=jnp.int32))
    query_back = jnp.moveaxis(query_parts, 0, 1).reshape(length, 1, own_width)
    kv_back = jnp.stack(
        [jnp.moveaxis(key_parts, 0, 1), jnp.moveaxis(value_parts, 0, 1)], axis=1
    ).reshape(length, 2, own_width)
    query_home, kv_home = (
        lax.all_to_all(query_back, "seq", split_axis=0, concat_axis=2, tiled=True),
        lax.all_to_all(kv_back, "seq", split_axis=0, concat_axis=2, tiled=True),
    )
    query_grad = query_home.reshape(1, tok_rows, HEADS * HEAD_DIM)
    one_hot = (head_slot[:, None] == jnp.arange(KV_SLOTS, dtype=jnp.int32)[None, :]).astype(
        jnp.bfloat16
    )
    summed = jnp.einsum(
        "tchd,hg->tcgd",
        kv_home.reshape(tok_rows, 2, HEADS, HEAD_DIM),
        one_hot,
        preferred_element_type=jnp.float32,
    ).astype(jnp.bfloat16)
    key_grad = summed[:, 0].reshape(1, tok_rows, KV_SLOTS * HEAD_DIM)
    value_grad = summed[:, 1].reshape(1, tok_rows, KV_SLOTS * HEAD_DIM)
    return (query_grad, key_grad, value_grad)


def solution(mesh):
    in_specs = (
        P("dp", "seq", None),
        P("dp", "seq", None),
        P("dp", "seq", None),
        P("dp", "seq", None),
        P("dp", "seq", None),
        P("dp", "seq"),
        P("dp"),
        P(),
    )
    out_specs = (P("dp", "seq", None), P("dp", "seq", None), P("dp", "seq", None))
    return jax.shard_map(local, mesh=mesh, in_specs=in_specs, out_specs=out_specs, check_vma=False)
```

profile of v0, /device:TPU:3, one launch (start us, length us, event | category | flops | bytes accessed | tf_op | source)
XLA Modules:
  0.0 383.1 jit_solution(5441480208483565896)
XLA Ops:
  17.7 15.3 %all-to-all-done.1 = bf16[128,8,512]{0,2,1:T(8,128)(2,1)S(1)} async-done(((bf16[128,8,512]{0,2,1:T(8,128)(2,1)}), bf16[128,8,512]{0,2,1:T(8,128)(2,1)S(1)}, u32[]{:S(2)}, u32[]{:S(2)}) %all-to-all-start.1) | async-done | bytes 1048608 | tf_op jit(solution)/shard_map/all_to_all | solution.py:145
  40.4 14.7 %all-to-all-done.2 = bf16[128,8,512]{0,2,1:T(8,128)(2,1)S(1)} async-done(((bf16[128,8,512]{0,2,1:T(8,128)(2,1)}), bf16[128,8,512]{0,2,1:T(8,128)(2,1)S(1)}, u32[]{:S(2)}, u32[]{:S(2)}) %all-to-all-start.2) | async-done | bytes 1048608 | tf_op jit(solution)/shard_map/all_to_all | solution.py:146
  61.5 10.8 %psum.7 = f32[]{:T(128)} all-reduce(f32[]{:T(128)} %bitcast.19), channel_id=1, replica_groups=mesh['seq'=8,'dp'=4] {'dp'}, use_global_device_ids=true, to_apply=%region_1.0 | all-reduce | flops 1 | bytes 8 | tf_op jit(solution)/shard_map/psum | solution.py:138
  73.0 10.9 %all-gather = s32[1,1024]{1,0:T(1,128)S(1)} all-gather(s32[1,128]{1,0:T(1,128)S(1)} %copy-done.6), channel_id=2, replica_groups=mesh['seq'=8,'dp'=4] {'seq'}, dimensions={1}, use_global_device_ids=true | all-gather | bytes 4608 | tf_op jit(solution)/shard_map/all_gather | solution.py:140
  103.1 209.0 %while.147 = (s32[]{:T(128)}, bf16[4,1024,128]{1,2,0:T(8,128)(2,1)}, bf16[4,1024,128]{1,2,0:T(8,128)(2,1)}, bf16[4,1024,128]{1,2,0:T(8,128)(2,1)}, f32[]{:T(128)...) while((s32[]{:T(128)}, bf16[4,1024,128]{1,2,0:T(8,128)(2,1)}, ...), condition=%wide.region_17.18_spmd, body=%wide.region_2.17_spmd.sunk | while | flops 409669152 | bytes 29343804 | solution.py:178
  107.8 18.2 %while.148 = (s32[]{:T(128)}, f32[2,512]{1,0:T(2,128)S(1)}, s32[2]{0:T(128)S(1)}, bf16[1024,128]{1,0:T(8,128)(2,1)S(1)}, s32[1024]{0:T(1024)S(1)}, /*index=5*/bf...) while((s32[]{:T(128)}, f32[2,512]{1,0:T(2,128)S(1)}, ...), condition=%wide.region_10.10_spmd, body=%wide.region_3.9_spmd.sunk | while | flops 70257176 | bytes 2691856 | solution.py:82
  109.7 6.4 %while.150 = (s32[]{:T(128)}, f32[512]{0:T(512)S(1)}, f32[512]{0:T(512)S(1)}, s32[]{:T(128)}, s32[1024]{0:T(1024)S(1)}, /*index=5*/s32[1]{0:T(128)}, bf16[1024,1...) while((s32[]{:T(128)}, f32[512]{0:T(512)S(1)}, ...), condition=%wide.region_9.8_spmd, body=%wide.region_4.7_spmd.sunk | while | flops 70256656 | bytes 2415021 | solution.py:77
  118.1 7.8 %while.150 = (s32[]{:T(128)}, f32[512]{0:T(512)S(1)}, f32[512]{0:T(512)S(1)}, s32[]{:T(128)}, s32[1024]{0:T(1024)S(1)}, /*index=5*/s32[1]{0:T(128)}, bf16[1024,1...) while((s32[]{:T(128)}, f32[512]{0:T(512)S(1)}, ...), condition=%wide.region_9.8_spmd, body=%wide.region_4.7_spmd.sunk | while | flops 70256656 | bytes 2415021 | solution.py:77
  127.3 25.2 %while.149 = (s32[]{:T(128)}, f32[1024,128]{1,0:T(8,128)S(1)}, f32[1024,128]{1,0:T(8,128)S(1)}, f32[2,512,128]{2,1,0:T(8,128)S(1)}, s32[2]{0:T(128)S(1)}, /*inde...) while((s32[]{:T(128)}, f32[1024,128]{1,0:T(8,128)S(1)}, ...), condition=%wide.region_16.16_spmd, body=%wide.region_11.15_spmd.sunk | while | flops 338625536 | bytes 8553470 | solution.py:128
  131.3 7.4 %while.151 = (s32[]{:T(128)}, f32[512,128]{1,0:T(8,128)S(1)}, f32[1024,128]{1,0:T(8,128)S(1)}, f32[1024,128]{1,0:T(8,128)S(1)}, s32[]{:T(128)}, /*index=5*/s32[1...) while((s32[]{:T(128)}, f32[512,128]{1,0:T(8,128)S(1)}, ...), condition=%wide.region_15.14_spmd, body=%wide.region_12.13_spmd.sunk | while | flops 338625536 | bytes 7234077 | solution.py:122
  142.6 9.9 %while.151 = (s32[]{:T(128)}, f32[512,128]{1,0:T(8,128)S(1)}, f32[1024,128]{1,0:T(8,128)S(1)}, f32[1024,128]{1,0:T(8,128)S(1)}, s32[]{:T(128)}, /*index=5*/s32[1...) while((s32[]{:T(128)}, f32[512,128]{1,0:T(8,128)S(1)}, ...), condition=%wide.region_15.14_spmd, body=%wide.region_12.13_spmd.sunk | while | flops 338625536 | bytes 7234077 | solution.py:122
  160.1 18.2 %while.148 = (s32[]{:T(128)}, f32[2,512]{1,0:T(2,128)S(1)}, s32[2]{0:T(128)S(1)}, bf16[1024,128]{1,0:T(8,128)(2,1)S(1)}, s32[1024]{0:T(1024)S(1)}, /*index=5*/bf...) while((s32[]{:T(128)}, f32[2,512]{1,0:T(2,128)S(1)}, ...), condition=%wide.region_10.10_spmd, body=%wide.region_3.9_spmd.sunk | while | flops 70257176 | bytes 2691856 | solution.py:82
  162.0 6.4 %while.150 = (s32[]{:T(128)}, f32[512]{0:T(512)S(1)}, f32[512]{0:T(512)S(1)}, s32[]{:T(128)}, s32[1024]{0:T(1024)S(1)}, /*index=5*/s32[1]{0:T(128)}, bf16[1024,1...) while((s32[]{:T(128)}, f32[512]{0:T(512)S(1)}, ...), condition=%wide.region_9.8_spmd, body=%wide.region_4.7_spmd.sunk | while | flops 70256656 | bytes 2415021 | solution.py:77
  170.4 7.8 %while.150 = (s32[]{:T(128)}, f32[512]{0:T(512)S(1)}, f32[512]{0:T(512)S(1)}, s32[]{:T(128)}, s32[1024]{0:T(1024)S(1)}, /*index=5*/s32[1]{0:T(128)}, bf16[1024,1...) while((s32[]{:T(128)}, f32[512]{0:T(512)S(1)}, ...), condition=%wide.region_9.8_spmd, body=%wide.region_4.7_spmd.sunk | while | flops 70256656 | bytes 2415021 | solution.py:77
  179.6 25.2 %while.149 = (s32[]{:T(128)}, f32[1024,128]{1,0:T(8,128)S(1)}, f32[1024,128]{1,0:T(8,128)S(1)}, f32[2,512,128]{2,1,0:T(8,128)S(1)}, s32[2]{0:T(128)S(1)}, /*inde...) while((s32[]{:T(128)}, f32[1024,128]{1,0:T(8,128)S(1)}, ...), condition=%wide.region_16.16_spmd, body=%wide.region_11.15_spmd.sunk | while | flops 338625536 | bytes 8553470 | solution.py:128
  183.5 7.4 %while.151 = (s32[]{:T(128)}, f32[512,128]{1,0:T(8,128)S(1)}, f32[1024,128]{1,0:T(8,128)S(1)}, f32[1024,128]{1,0:T(8,128)S(1)}, s32[]{:T(128)}, /*index=5*/s32[1...) while((s32[]{:T(128)}, f32[512,128]{1,0:T(8,128)S(1)}, ...), condition=%wide.region_15.14_spmd, body=%wide.region_12.13_spmd.sunk | while | flops 338625536 | bytes 7234077 | solution.py:122
  194.9 9.9 %while.151 = (s32[]{:T(128)}, f32[512,128]{1,0:T(8,128)S(1)}, f32[1024,128]{1,0:T(8,128)S(1)}, f32[1024,128]{1,0:T(8,128)S(1)}, s32[]{:T(128)}, /*index=5*/s32[1...) while((s32[]{:T(128)}, f32[512,128]{1,0:T(8,128)S(1)}, ...), condition=%wide.region_15.14_spmd, body=%wide.region_12.13_spmd.sunk | while | flops 338625536 | bytes 7234077 | solution.py:122
  212.3 18.2 %while.148 = (s32[]{:T(128)}, f32[2,512]{1,0:T(2,128)S(1)}, s32[2]{0:T(128)S(1)}, bf16[1024,128]{1,0:T(8,128)(2,1)S(1)}, s32[1024]{0:T(1024)S(1)}, /*index=5*/bf...) while((s32[]{:T(128)}, f32[2,512]{1,0:T(2,128)S(1)}, ...), condition=%wide.region_10.10_spmd, body=%wide.region_3.9_spmd.sunk | while | flops 70257176 | bytes 2691856 | solution.py:82
  214.2 6.4 %while.150 = (s32[]{:T(128)}, f32[512]{0:T(512)S(1)}, f32[512]{0:T(512)S(1)}, s32[]{:T(128)}, s32[1024]{0:T(1024)S(1)}, /*index=5*/s32[1]{0:T(128)}, bf16[1024,1...) while((s32[]{:T(128)}, f32[512]{0:T(512)S(1)}, ...), condition=%wide.region_9.8_spmd, body=%wide.region_4.7_spmd.sunk | while | flops 70256656 | bytes 2415021 | solution.py:77
  222.6 7.8 %while.150 = (s32[]{:T(128)}, f32[512]{0:T(512)S(1)}, f32[512]{0:T(512)S(1)}, s32[]{:T(128)}, s32[1024]{0:T(1024)S(1)}, /*index=5*/s32[1]{0:T(128)}, bf16[1024,1...) while((s32[]{:T(128)}, f32[512]{0:T(512)S(1)}, ...), condition=%wide.region_9.8_spmd, body=%wide.region_4.7_spmd.sunk | while | flops 70256656 | bytes 2415021 | solution.py:77
  231.8 25.2 %while.149 = (s32[]{:T(128)}, f32[1024,128]{1,0:T(8,128)S(1)}, f32[1024,128]{1,0:T(8,128)S(1)}, f32[2,512,128]{2,1,0:T(8,128)S(1)}, s32[2]{0:T(128)S(1)}, /*inde...) while((s32[]{:T(128)}, f32[1024,128]{1,0:T(8,128)S(1)}, ...), condition=%wide.region_16.16_spmd, body=%wide.region_11.15_spmd.sunk | while | flops 338625536 | bytes 8553470 | solution.py:128
  235.8 7.4 %while.151 = (s32[]{:T(128)}, f32[512,128]{1,0:T(8,128)S(1)}, f32[1024,128]{1,0:T(8,128)S(1)}, f32[1024,128]{1,0:T(8,128)S(1)}, s32[]{:T(128)}, /*index=5*/s32[1...) while((s32[]{:T(128)}, f32[512,128]{1,0:T(8,128)S(1)}, ...), condition=%wide.region_15.14_spmd, body=%wide.region_12.13_spmd.sunk | while | flops 338625536 | bytes 7234077 | solution.py:122
  247.1 9.9 %while.151 = (s32[]{:T(128)}, f32[512,128]{1,0:T(8,128)S(1)}, f32[1024,128]{1,0:T(8,128)S(1)}, f32[1024,128]{1,0:T(8,128)S(1)}, s32[]{:T(128)}, /*index=5*/s32[1...) while((s32[]{:T(128)}, f32[512,128]{1,0:T(8,128)S(1)}, ...), condition=%wide.region_15.14_spmd, body=%wide.region_12.13_spmd.sunk | while | flops 338625536 | bytes 7234077 | solution.py:122
  264.5 18.2 %while.148 = (s32[]{:T(128)}, f32[2,512]{1,0:T(2,128)S(1)}, s32[2]{0:T(128)S(1)}, bf16[1024,128]{1,0:T(8,128)(2,1)S(1)}, s32[1024]{0:T(1024)S(1)}, /*index=5*/bf...) while((s32[]{:T(128)}, f32[2,512]{1,0:T(2,128)S(1)}, ...), condition=%wide.region_10.10_spmd, body=%wide.region_3.9_spmd.sunk | while | flops 70257176 | bytes 2691856 | solution.py:82
  266.5 6.4 %while.150 = (s32[]{:T(128)}, f32[512]{0:T(512)S(1)}, f32[512]{0:T(512)S(1)}, s32[]{:T(128)}, s32[1024]{0:T(1024)S(1)}, /*index=5*/s32[1]{0:T(128)}, bf16[1024,1...) while((s32[]{:T(128)}, f32[512]{0:T(512)S(1)}, ...), condition=%wide.region_9.8_spmd, body=%wide.region_4.7_spmd.sunk | while | flops 70256656 | bytes 2415021 | solution.py:77
  274.9 7.8 %while.150 = (s32[]{:T(128)}, f32[512]{0:T(512)S(1)}, f32[512]{0:T(512)S(1)}, s32[]{:T(128)}, s32[1024]{0:T(1024)S(1)}, /*index=5*/s32[1]{0:T(128)}, bf16[1024,1...) while((s32[]{:T(128)}, f32[512]{0:T(512)S(1)}, ...), condition=%wide.region_9.8_spmd, body=%wide.region_4.7_spmd.sunk | while | flops 70256656 | bytes 2415021 | solution.py:77
  284.1 25.2 %while.149 = (s32[]{:T(128)}, f32[1024,128]{1,0:T(8,128)S(1)}, f32[1024,128]{1,0:T(8,128)S(1)}, f32[2,512,128]{2,1,0:T(8,128)S(1)}, s32[2]{0:T(128)S(1)}, /*inde...) while((s32[]{:T(128)}, f32[1024,128]{1,0:T(8,128)S(1)}, ...), condition=%wide.region_16.16_spmd, body=%wide.region_11.15_spmd.sunk | while | flops 338625536 | bytes 8553470 | solution.py:128
  288.0 7.4 %while.151 = (s32[]{:T(128)}, f32[512,128]{1,0:T(8,128)S(1)}, f32[1024,128]{1,0:T(8,128)S(1)}, f32[1024,128]{1,0:T(8,128)S(1)}, s32[]{:T(128)}, /*index=5*/s32[1...) while((s32[]{:T(128)}, f32[512,128]{1,0:T(8,128)S(1)}, ...), condition=%wide.region_15.14_spmd, body=%wide.region_12.13_spmd.sunk | while | flops 338625536 | bytes 7234077 | solution.py:122
  299.3 9.9 %while.151 = (s32[]{:T(128)}, f32[512,128]{1,0:T(8,128)S(1)}, f32[1024,128]{1,0:T(8,128)S(1)}, f32[1024,128]{1,0:T(8,128)S(1)}, s32[]{:T(128)}, /*index=5*/s32[1...) while((s32[]{:T(128)}, f32[512,128]{1,0:T(8,128)S(1)}, ...), condition=%wide.region_15.14_spmd, body=%wide.region_12.13_spmd.sunk | while | flops 338625536 | bytes 7234077 | solution.py:122
  327.7 8.1 %all-to-all-done.3 = bf16[8,2,32768]{2,1,0:T(2,128)(2,1)} async-done(((bf16[8,2,32768]{2,1,0:T(2,128)(2,1)}), bf16[8,2,32768]{2,1,0:T(2,128)(2,1)}, u32[]{:S(2)}, u32[]{:S(2)}) %all-to-all-start.3) | async-done | bytes 1048608 | tf_op jit(solution)/shard_map/all_to_all | solution.py:184
  335.8 5.8 %all-to-all-start.4 = ((bf16[1024,2,512]{2,1,0:T(2,128)(2,1)}), bf16[1024,2,512]{2,1,0:T(2,128)(2,1)}, u32[]{:S(2)}, u32[]{:S(2)}) async-start(bf16[1024,2,512]{2,1,0:T(2,128)(2,1)} %copy.60), calls=%async_computation.4 | async-start | bytes 4194304 | tf_op jit(solution)/shard_map/all_to_all | solution.py:185
  350.1 16.7 %all-to-all-done.4 = bf16[1024,2,512]{2,1,0:T(2,128)(2,1)} async-done(((bf16[1024,2,512]{2,1,0:T(2,128)(2,1)}), bf16[1024,2,512]{2,1,0:T(2,128)(2,1)}, u32[]{:S(2)}, u32[]{:S(2)}) %all-to-all-start.4) | async-done | bytes 2097184 | tf_op jit(solution)/shard_map/all_to_all | solution.py:185
  (508 shorter events, 223.2 us)
Async XLA Ops:
  7.2 3.2 copy-start.2
  7.2 92.0 %all-gather.3.cloned.1.call-start = ((), (), s32[]{:S(2)}) async-start(), calls=%async_computation.5 | async-start | bytes 2359296 | tf_op jit(solution)/shard_map/all_gather | solution.py:151
  11.7 4.7 %copy-start.3 = (bf16[1,128,4096]{2,1,0:T(8,128)(2,1)S(1)}, bf16[1,128,4096]{2,1,0:T(8,128)(2,1)}, u32[]{:S(2)}) copy-start(bf16[1,128,4096]{2,1,0:T(8,128)(2,1)} %param.25) | copy-start | bytes 3145732
  11.7 21.3 %all-to-all-start.1 = ((bf16[128,8,512]{0,2,1:T(8,128)(2,1)}), bf16[128,8,512]{0,2,1:T(8,128)(2,1)S(1)}, u32[]{:S(2)}, u32[]{:S(2)}) async-start(bf16[128,8,512]{0,2,1:T(8,128)(2,1)} %bitcast.22), calls=%async_computation.1 | async-start | bytes 2097152 | tf_op jit(solution)/shard_map/all_to_all | solution.py:145
  33.0 22.0 %all-to-all-start.2 = ((bf16[128,8,512]{0,2,1:T(8,128)(2,1)}), bf16[128,8,512]{0,2,1:T(8,128)(2,1)S(1)}, u32[]{:S(2)}, u32[]{:S(2)}) async-start(bf16[128,8,512]{0,2,1:T(8,128)(2,1)} %bitcast.132), calls=%async_computation.2 | async-start | bytes 2097152 | tf_op jit(solution)/shard_map/all_to_all | solution.py:146
  38.1 34.9 %copy-start.6 = (s32[1,128]{1,0:T(1,128)S(1)}, s32[1,128]{1,0:T(1,128)}, u32[]{:S(2)}) copy-start(s32[1,128]{1,0:T(1,128)} %param.27) | copy-start | bytes 1540
  38.1 45.9 %copy-start.4 = (s32[32]{0:T(128)S(1)}, s32[32]{0:T(128)}, u32[]{:S(2)}) copy-start(s32[32]{0:T(128)} %param.29) | copy-start | bytes 388
  55.1 37.3 %all-to-all-start = ((bf16[128,8,512]{0,2,1:T(8,128)(2,1)}), bf16[128,8,512]{0,2,1:T(8,128)(2,1)}, u32[]{:S(2)}, u32[]{:S(2)}) async-start(bf16[128,8,512]{0,2,1:T(8,128)(2,1)} %bitcast.131), calls=%async_computation | async-start | bytes 2097152 | tf_op jit(solution)/shard_map/all_to_all | solution.py:144
  103.1 24.1 %copy-start = (bf16[1024,4,128]{2,0,1:T(8,128)(2,1)}, bf16[1024,4,128]{2,0,1:T(8,128)(2,1)S(1)}, u32[]{:S(2)}) copy-start(bf16[1024,4,128]{2,0,1:T(8,128)(2,1)S(1)} %get-tuple-element.2153) | copy-start | bytes 3145732 | tf_op jit(solution)/shard_map/while
  152.6 2.7 copy-start.1
  155.3 24.1 %copy-start = (bf16[1024,4,128]{2,0,1:T(8,128)(2,1)}, bf16[1024,4,128]{2,0,1:T(8,128)(2,1)S(1)}, u32[]{:S(2)}) copy-start(bf16[1024,4,128]{2,0,1:T(8,128)(2,1)S(1)} %get-tuple-element.2153) | copy-start | bytes 3145732 | tf_op jit(solution)/shard_map/while
  204.9 2.7 copy-start.1
  207.6 24.1 %copy-start = (bf16[1024,4,128]{2,0,1:T(8,128)(2,1)}, bf16[1024,4,128]{2,0,1:T(8,128)(2,1)S(1)}, u32[]{:S(2)}) copy-start(bf16[1024,4,128]{2,0,1:T(8,128)(2,1)S(1)} %get-tuple-element.2153) | copy-start | bytes 3145732 | tf_op jit(solution)/shard_map/while
  257.1 2.7 copy-start.1
  259.8 24.1 %copy-start = (bf16[1024,4,128]{2,0,1:T(8,128)(2,1)}, bf16[1024,4,128]{2,0,1:T(8,128)(2,1)S(1)}, u32[]{:S(2)}) copy-start(bf16[1024,4,128]{2,0,1:T(8,128)(2,1)S(1)} %get-tuple-element.2153) | copy-start | bytes 3145732 | tf_op jit(solution)/shard_map/while
  309.3 2.7 copy-start.1
  317.4 18.4 %all-to-all-start.3 = ((bf16[8,2,32768]{2,1,0:T(2,128)(2,1)}), bf16[8,2,32768]{2,1,0:T(2,128)(2,1)}, u32[]{:S(2)}, u32[]{:S(2)}) async-start(bf16[8,2,32768]{2,1,0:T(2,128)(2,1)} %reshape.109), calls=%async_computation.3 | async-start | bytes 2097152 | tf_op jit(solution)/shard_map/all_to_all | solution.py:184
  335.8 31.0 %all-to-all-start.4 = ((bf16[1024,2,512]{2,1,0:T(2,128)(2,1)}), bf16[1024,2,512]{2,1,0:T(2,128)(2,1)}, u32[]{:S(2)}, u32[]{:S(2)}) async-start(bf16[1024,2,512]{2,1,0:T(2,128)(2,1)} %copy.60), calls=%async_computation.4 | async-start | bytes 4194304 | tf_op jit(solution)/shard_map/all_to_all | solution.py:185
  371.2 3.1 copy-start.5
Sparse Core Ops, SparseCore 0:
  10.5 44.1 all-gather.2
where the time goes:
time: 388 us; the launch traced here: 383 us
  local copies, waits for them, and re-layouts  118 us (30%)
  loops' own time  110 us (28%)
  waiting for transfers between devices  54.8 us (14%)
  starting transfers between devices  25.8 us (7%)
  matrix products  25.6 us (7%)
  blocking collectives  21.7 us (6%)
  between operations  15.5 us (4%)
  other arithmetic  11.9 us (3%)
    another operation x8, loops' own time, query_pass(): lax.fori_loop(jnp.int32(0), jnp.int32(tile_count), query_visit_tile, star...  29.7 us
    another operation x8, loops' own time, row_stats(): lax.fori_loop(jnp.int32(0), jnp.int32(tile_count), row_visit_tile, start_...  29.7 us
    another operation x4, loops' own time, head_grads(): lax.scan(query_pass, (zero_rows, zero_rows), tiles)  20.4 us
    dynamic_slice x32, local copies, waits for them, and re-layouts, tile_live(): lax.dynamic_index_in_dim(doc_ids, k_tile * tile_rows + tile_rows - 1, 0,...  18.8 us
    all_to_all x1, waiting for transfers between devices, local(): lax.all_to_all(kv_back, 'seq', split_axis=0, concat_axis=2, tiled=True)  16.7 us
    unnamed x20, local copies, waits for them, and re-layouts  16.1 us
    all_to_all x1, waiting for transfers between devices, local(): lax.all_to_all(grad_rows, 'seq', split_axis=1, concat_axis=0, tiled=True)  15.3 us
    all_to_all x1, waiting for transfers between devices, local(): lax.all_to_all(attn_out[0], 'seq', split_axis=1, concat_axis=0, tiled=True)  14.7 us
  transfers between devices with their start and end apart: 6, of which 4 were waited for; matrix products, arithmetic and copies ran while one was open for 9% of the time, Pallas kernels for 0%

commit v1 on v0

v1 whole, which is shorter than its diff:
```python
import functools
import math

import jax
import jax.numpy as jnp
from jax import lax
from jax.experimental import pallas as pl
from jax.experimental.pallas import tpu as pltpu
from jax.sharding import PartitionSpec as P

HEADS = 32
HEAD_DIM = 128
KV_SLOTS = 4
WIDTH = HEADS * HEAD_DIM
KV_WIDTH = KV_SLOTS * HEAD_DIM
NEG_FILL = -1e30
SCALE = 1.0 / math.sqrt(HEAD_DIM)
EXP2_SCALE = SCALE / math.log(2.0)
MESH = pl.DeviceIdType.MESH


def dot(left, right, dims):
    return lax.dot_general(left, right, (dims, ((), ())), preferred_element_type=jnp.float32)


def block_diag(both):
    first, second = both[:, :HEAD_DIM], both[:, HEAD_DIM:]
    zero = jnp.zeros_like(first)
    return jnp.concatenate(
        [jnp.concatenate([first, zero], axis=1), jnp.concatenate([zero, second], axis=1)], axis=0
    )


def kernel(
    n, ndp, rows,
    q_hbm, k_hbm, v_hbm, o_hbm, g_hbm, seg_ref, cnt_ref, slot_ref,
    dq_ref, dk_ref, dv_ref,
    qbuf, gbuf, obuf, kbuf, vbuf, kslot, vslot, ktslot, sbuf, cbuf, bias,
    acc_k, acc_v, back, home,
    local_sem, kv_send, kv_recv, cnt_send, cnt_recv, back_send, back_recv,
):
    halo = n // 4
    me = lax.axis_index("seq")
    my_dp = lax.axis_index("dp")

    loads = [
        pltpu.make_async_copy(k_hbm, kbuf.at[pl.ds(halo * rows, rows)], local_sem.at[0]),
        pltpu.make_async_copy(v_hbm, vbuf.at[pl.ds(halo * rows, rows)], local_sem.at[1]),
        pltpu.make_async_copy(q_hbm, qbuf, local_sem.at[2]),
        pltpu.make_async_copy(g_hbm, gbuf, local_sem.at[3]),
        pltpu.make_async_copy(o_hbm, obuf, local_sem.at[4]),
    ]
    for load in loads:
        load.start()

    barrier = pltpu.get_barrier_semaphore()
    for j in range(1, halo + 1):
        for other in (me + j, me - j):
            @pl.when(jnp.logical_and(other >= 0, other < n))
            def _():
                pl.semaphore_signal(barrier, inc=1, device_id={"seq": other}, device_id_type=MESH)
    for j in range(1, ndp):
        pl.semaphore_signal(
            barrier, inc=1, device_id={"dp": lax.rem(my_dp + j, ndp)}, device_id_type=MESH
        )
    pl.semaphore_wait(
        barrier, jnp.minimum(me, halo) + jnp.minimum(n - 1 - me, halo) + (ndp - 1)
    )

    def halo_copies(j):
        target = {"seq": me + j}
        place = pl.ds((halo - j) * rows, rows)
        return [
            pltpu.make_async_remote_copy(
                src, dst, kv_send.at[j - 1, i], kv_recv.at[j - 1, i],
                device_id=target, device_id_type=MESH,
            )
            for i, (src, dst) in enumerate(
                [
                    (k_hbm, kbuf.at[place]),
                    (v_hbm, vbuf.at[place]),
                    (seg_ref, sbuf.at[halo - j]),
                ]
            )
        ]

    for j in range(halo, 0, -1):
        @pl.when(me + j < n)
        def _():
            for copy in halo_copies(j):
                copy.start()

    cbuf[0] = jnp.full((8, 128), cnt_ref[0].astype(jnp.float32))

    def count_copy(j):
        return pltpu.make_async_remote_copy(
            cbuf.at[0], cbuf.at[j], cnt_send.at[j], cnt_recv.at[j],
            device_id={"dp": lax.rem(my_dp + j, ndp)}, device_id_type=MESH,
        )

    for j in range(1, ndp):
        count_copy(j).start()

    sbuf[halo] = seg_ref[...]
    for j in range(1, halo + 1):
        @pl.when(me - j < 0)
        def _():
            kbuf[pl.ds((halo - j) * rows, rows), :] = jnp.zeros((rows, KV_WIDTH), jnp.bfloat16)
            vbuf[pl.ds((halo - j) * rows, rows), :] = jnp.zeros((rows, KV_WIDTH), jnp.bfloat16)
            sbuf[halo - j] = jnp.full((1, rows), -1, jnp.int32)

    for load in loads:
        load.wait()
    for j in range(1, ndp):
        count_copy(j).wait_recv()
    for j in range(1, halo + 1):
        @pl.when(me - j >= 0)
        def _():
            for copy in halo_copies(j):
                copy.wait_recv()

    total = cbuf[0]
    for j in range(1, ndp):
        total = total + cbuf[j]
    factor = (float(ndp * n * rows) / total)[0:1, :]
    scaled = factor * SCALE

    q_doc = seg_ref[...].astype(jnp.float32)
    for b in range(halo + 1):
        k_doc = jnp.transpose(jnp.broadcast_to(sbuf[b].astype(jnp.float32), (rows, rows)))
        allowed = k_doc == q_doc
        if b == halo:
            k_pos = lax.broadcasted_iota(jnp.int32, (rows, rows), 0)
            q_pos = lax.broadcasted_iota(jnp.int32, (rows, rows), 1)
            allowed = jnp.logical_and(allowed, k_pos <= q_pos)
        one = jnp.where(allowed, 0.0, NEG_FILL)
        place = pl.ds(b * rows, rows)
        bias[place, :] = jnp.concatenate([one, one], axis=1)
        for s in range(KV_SLOTS):
            lanes = pl.ds(s * HEAD_DIM, HEAD_DIM)
            tile = kbuf[place, lanes]
            kslot[s, place, :] = tile
            ktslot[s, :, place] = jnp.transpose(tile)
            vslot[s, place, :] = vbuf[place, lanes]

    def pair(p, carry):
        h1 = 2 * p
        h2 = h1 + 1
        s1, s2 = slot_ref[h1], slot_ref[h2]
        before = slot_ref[lax.rem(h1 + HEADS - 1, HEADS)]
        keep1 = jnp.where(before == s1, 1.0, 0.0)
        keep2 = jnp.where(s1 == s2, 1.0, 0.0)
        cols = pl.ds(pl.multiple_of(p * 2 * HEAD_DIM, 2 * HEAD_DIM), 2 * HEAD_DIM)
        q2, g2, o2 = qbuf[:, cols], gbuf[:, cols], obuf[:, cols]
        q_diag, g_diag = block_diag(q2), block_diag(g2)
        k_cat = jnp.concatenate([kslot[s1], kslot[s2]], axis=1)
        v_cat = jnp.concatenate([vslot[s1], vslot[s2]], axis=1)

        product = g2.astype(jnp.float32) * o2.astype(jnp.float32)
        high = product.astype(jnp.bfloat16)
        low = (product - high.astype(jnp.float32)).astype(jnp.bfloat16)
        terms = jnp.concatenate(
            [
                jnp.concatenate([high[:, :HEAD_DIM], low[:, :HEAD_DIM]], axis=1),
                jnp.concatenate([high[:, HEAD_DIM:], low[:, HEAD_DIM:]], axis=1),
            ],
            axis=0,
        )
        ones = jnp.ones((16, 2 * HEAD_DIM), jnp.bfloat16)
        delta = dot(ones, terms, ((1,), (1,)))[0:1, :]

        scores = dot(k_cat, q_diag, ((1,), (1,))) + bias[...]
        top = jnp.max(scores, axis=0, keepdims=True)
        expd = jnp.exp2((scores - top) * EXP2_SCALE)
        weights = expd * (1.0 / jnp.sum(expd, axis=0, keepdims=True))
        grad_weights = dot(v_cat, g_diag, ((1,), (1,)))
        score_grad = (weights * (grad_weights - delta)).astype(jnp.bfloat16)

        v_part = dot(weights.astype(jnp.bfloat16), g_diag, ((1,), (0,)))
        k_part = dot(score_grad, q_diag, ((1,), (0,)))
        for acc, part in ((acc_k, k_part), (acc_v, v_part)):
            first = acc[h1] * keep1 + part[:, :HEAD_DIM]
            acc[h1 + 1] = first
            acc[h1 + 2] = first * keep2 + part[:, HEAD_DIM:]

        turned = []
        for i, s in enumerate((s1, s2)):
            dqt = dot(ktslot[s], score_grad[:, i * HEAD_DIM:(i + 1) * HEAD_DIM], ((1,), (0,)))
            turned.append((jnp.transpose(dqt) * scaled).astype(jnp.bfloat16))
        dq_ref[:, cols] = jnp.concatenate(turned, axis=1)
        return carry

    acc_k[0] = jnp.zeros(acc_k.shape[1:], jnp.float32)
    acc_v[0] = jnp.zeros(acc_v.shape[1:], jnp.float32)
    lax.fori_loop(0, HEADS // 2, pair, 0)

    lasts = [jnp.int32(0)] * KV_SLOTS
    for h in range(HEADS):
        slot = slot_ref[h]
        lasts = [last + (slot <= s).astype(jnp.int32) for s, last in enumerate(lasts)]

    def back_copy(j):
        return pltpu.make_async_remote_copy(
            back.at[j - 1], home.at[j - 1], back_send.at[j - 1], back_recv.at[j - 1],
            device_id={"seq": me - j}, device_id_type=MESH,
        )

    for j in range(halo, 0, -1):
        place = pl.ds((halo - j) * rows, rows)
        for s in range(KV_SLOTS):
            lanes = pl.ds(s * HEAD_DIM, HEAD_DIM)
            back[j - 1, 0, :, lanes] = (acc_k[lasts[s], place, :] * scaled).astype(jnp.bfloat16)
            back[j - 1, 1, :, lanes] = (acc_v[lasts[s], place, :] * factor).astype(jnp.bfloat16)

        @pl.when(me - j >= 0)
        def _():
            back_copy(j).start()

    for j in range(1, halo + 1):
        @pl.when(me + j >= n)
        def _():
            home[j - 1] = jnp.zeros(home.shape[1:], jnp.bfloat16)

        @pl.when(me + j < n)
        def _():
            back_copy(j).wait_recv()

    place = pl.ds(halo * rows, rows)
    for s in range(KV_SLOTS):
        lanes = pl.ds(s * HEAD_DIM, HEAD_DIM)
        for i, (acc, gain, out) in enumerate(((acc_k, scaled, dk_ref), (acc_v, factor, dv_ref))):
            value = acc[lasts[s], place, :] * gain
            for j in range(halo):
                value = value + home[j, i, :, lanes].astype(jnp.float32)
            out[:, lanes] = value.astype(jnp.bfloat16)

    for j in range(1, ndp):
        count_copy(j).wait_send()
    for j in range(1, halo + 1):
        @pl.when(me + j < n)
        def _():
            for copy in halo_copies(j):
                copy.wait_send()

        @pl.when(me - j >= 0)
        def _():
            back_copy(j).wait_send()


def local(queries, keys, values, attn_out, out_grad, segments, token_counts, head_slot):
    n, ndp = lax.axis_size("seq"), lax.axis_size("dp")
    rows = queries.shape[1]
    halo = n // 4
    span = (halo + 1) * rows
    hbm = pl.BlockSpec(memory_space=pl.ANY)
    vmem = pl.BlockSpec(memory_space=pltpu.VMEM)
    smem = pl.BlockSpec(memory_space=pltpu.SMEM)
    bf16, f32 = jnp.bfloat16, jnp.float32
    dma = pltpu.SemaphoreType.DMA
    dq, dk, dv = pl.pallas_call(
        functools.partial(kernel, n, ndp, rows),
        out_shape=[
            jax.ShapeDtypeStruct((rows, WIDTH), bf16),
            jax.ShapeDtypeStruct((rows, KV_WIDTH), bf16),
            jax.ShapeDtypeStruct((rows, KV_WIDTH), bf16),
        ],
        in_specs=[hbm] * 5 + [vmem, smem, smem],
        out_specs=[vmem] * 3,
        scratch_shapes=[
            pltpu.VMEM((rows, WIDTH), bf16),
            pltpu.VMEM((rows, WIDTH), bf16),
            pltpu.VMEM((rows, WIDTH), bf16),
            pltpu.VMEM((span, KV_WIDTH), bf16),
            pltpu.VMEM((span, KV_WIDTH), bf16),
            pltpu.VMEM((KV_SLOTS, span, HEAD_DIM), bf16),
            pltpu.VMEM((KV_SLOTS, span, HEAD_DIM), bf16),
            pltpu.VMEM((KV_SLOTS, HEAD_DIM, span), bf16),
            pltpu.VMEM((halo + 1, 1, rows), jnp.int32),
            pltpu.VMEM((ndp, 8, 128), f32),
            pltpu.VMEM((span, 2 * HEAD_DIM), f32),
            pltpu.VMEM((HEADS + 1, span, HEAD_DIM), f32),
            pltpu.VMEM((HEADS + 1, span, HEAD_DIM), f32),
            pltpu.VMEM((halo, 2, rows, KV_WIDTH), bf16),
            pltpu.VMEM((halo, 2, rows, KV_WIDTH), bf16),
            dma((5,)),
            dma((halo, 3)),
            dma((halo, 3)),
            dma((ndp,)),
            dma((ndp,)),
            dma((halo,)),
            dma((halo,)),
        ],
        compiler_params=pltpu.CompilerParams(
            collective_id=0, has_side_effects=True, vmem_limit_bytes=60 * 1024 * 1024
        ),
    )(queries[0], keys[0], values[0], attn_out[0], out_grad[0], segments, token_counts, head_slot)
    return dq[None], dk[None], dv[None]


def solution(mesh):
    in_specs = (
        P("dp", "seq", None),
        P("dp", "seq", None),
        P("dp", "seq", None),
        P("dp", "seq", None),
        P("dp", "seq", None),
        P("dp", "seq"),
        P("dp"),
        P(),
    )
    out_specs = (P("dp", "seq", None), P("dp", "seq", None), P("dp", "seq", None))
    return jax.shard_map(local, mesh=mesh, in_specs=in_specs, out_specs=out_specs, check_vma=False)
```

time: 388 us -> 44.3 us (0.11); the launches traced: 383 us -> 44.2 us
  local copies, waits for them, and re-layouts: 118 us -> 3.93 us
  loops' own time: 110 us -> 0 us
  waiting for transfers between devices: 54.8 us -> 0 us
  Pallas kernels: 0 us -> 38.9 us
  starting transfers between devices: 25.8 us -> 0 us
  matrix products: 25.6 us -> 0 us
  blocking collectives: 21.7 us -> 0 us
  between operations: 15.5 us -> 1.3 us
  other arithmetic: 11.9 us -> 0 us
    another operation x57 -> x0, loops' own time: 110 us -> none  [the longest x8 29.7 us: query_pass(): lax.fori_loop(jnp.int32(0), jnp.int32(tile_count), query_visit_tile, star...]
    all_to_all x5 -> x0, waiting for transfers between devices: 54.8 us -> none  [the longest x1 16.7 us: local(): lax.all_to_all(kv_back, 'seq', split_axis=0, concat_axis=2, tiled=True)]
    dynamic_slice x144 -> x0, local copies, waits for them, and re-layouts: 53.8 us -> none  [the longest x32 18.8 us: tile_live(): lax.dynamic_index_in_dim(doc_ids, k_tile * tile_rows + tile_rows - 1, 0,...]
    pallas_call x0 -> x1, Pallas kernels: none -> 38.9 us  [local(): pl.pallas_call(functools.partial(kernel, n, ndp, rows), out_shape=[jax.Sh...]
    all_to_all x5 -> x0, starting transfers between devices: 25.8 us -> none  [the longest x1 5.84 us: local(): lax.all_to_all(kv_back, 'seq', split_axis=0, concat_axis=2, tiled=True)]
    dot_general x73 -> x0, matrix products: 25.6 us -> none  [the longest x36 13.6 us: contract_rows(): lax.dot_general(left, right, (((1,), (1,)), ((), ())), preferred_element_...]
    unnamed x20 -> x7, local copies, waits for them, and re-layouts: 16.1 us -> 3.93 us
    dynamic_update_slice x40 -> x0, local copies, waits for them, and re-layouts: 11 us -> none  [the longest x24 10.5 us: local(): lax.map(one_head, jnp.arange(heads_dev, dtype=jnp.int32))]
  transfers between devices with their start and end apart: 6 -> 0, of which waited for: 4 -> 0; matrix products, arithmetic and copies ran while one was open for 9% -> 0% of each run, Pallas kernels for 0% -> 0%
where the time goes in v1:
time: 44.3 us; the launch traced here: 44.2 us
  Pallas kernels  38.9 us (88%)
  local copies, waits for them, and re-layouts  3.93 us (9%)
  between operations  1.3 us (3%)
    pallas_call x1, Pallas kernels, local(): pl.pallas_call(functools.partial(kernel, n, ndp, rows), out_shape=[jax.Sh...  38.9 us
    unnamed x7, local copies, waits for them, and re-layouts  3.93 us

profile of v1, /device:TPU:3, one launch (start us, length us, event | category | flops | bytes accessed | tf_op | source)
XLA Modules:
  0.0 44.2 jit_solution(11265079912618722245)
XLA Ops:
  1.3 38.9 %shard_map.103 = (bf16[128,4096]{1,0:T(8,128)(2,1)}, bf16[128,512]{1,0:T(8,128)(2,1)}, bf16[128,512]{1,0:T(8,128)(2,1)}) custom-call(bf16[128,4096]{1,0:T(8,128)(2,1)} %bitcast.9, bf16[128,512]{1,0:T(8,128)(2,1)} %bitcast.14, bf16[128,512]{1,0:T(8,128)(2,1)} %bitcast.15, bf16[128,4096]{1,0:T(8,128)(2,1)} %bitcast.10, bf16[128,4096]{1,0:T(8,128)(2,1)} %bitcast.11, ...), custom_call_target="tpu_custom_call" | custom-call | tf_op jit(solution)/shard_map/pallas_call | solution.py:260
  40.2 0.0 copy-start.1
  40.2 2.3 %copy.15 = bf16[1,128,4096]{2,1,0:T(8,128)(2,1)} copy(bf16[1,128,4096]{2,1,0:T(8,128)(2,1)} %bitcast.8) | data formatting | bytes 2097152
  42.5 0.0 copy-done.1
  42.5 0.0 copy-start
  42.5 0.7 %copy.16 = bf16[1,128,512]{2,1,0:T(8,128)(2,1)} copy(bf16[1,128,512]{2,1,0:T(8,128)(2,1)S(1)} %bitcast.13) | data formatting | bytes 262144
  43.2 0.3 copy-done
  43.5 0.7 %copy.17 = bf16[1,128,512]{2,1,0:T(8,128)(2,1)} copy(bf16[1,128,512]{2,1,0:T(8,128)(2,1)S(1)} %bitcast.12) | data formatting | bytes 262144
Async XLA Ops:
  40.2 2.3 %copy-start.1 = (bf16[128,512]{1,0:T(8,128)(2,1)S(1)}, bf16[128,512]{1,0:T(8,128)(2,1)}, u32[]{:S(2)}) copy-start(bf16[128,512]{1,0:T(8,128)(2,1)} %get-tuple-element.7) | copy-start | bytes 393220
  42.5 1.0 %copy-start = (bf16[128,512]{1,0:T(8,128)(2,1)S(1)}, bf16[128,512]{1,0:T(8,128)(2,1)}, u32[]{:S(2)}) copy-start(bf16[128,512]{1,0:T(8,128)(2,1)} %get-tuple-element.8) | copy-start | bytes 393220

commit v2 on v1

--- a/solution.py
+++ b/solution.py
@@ -17,6 +17,7 @@
 SCALE = 1.0 / math.sqrt(HEAD_DIM)
 EXP2_SCALE = SCALE / math.log(2.0)
 MESH = pl.DeviceIdType.MESH
+UNROLL = 4
 
 
 def dot(left, right, dims):
@@ -34,10 +35,11 @@
 def kernel(
     n, ndp, rows,
     q_hbm, k_hbm, v_hbm, o_hbm, g_hbm, seg_ref, cnt_ref, slot_ref,
-    dq_ref, dk_ref, dv_ref,
+    dq_hbm, dk_ref, dv_ref,
     qbuf, gbuf, obuf, kbuf, vbuf, kslot, vslot, ktslot, sbuf, cbuf, bias,
-    acc_k, acc_v, back, home,
-    local_sem, kv_send, kv_recv, cnt_send, cnt_recv, back_send, back_recv,
+    acc_k, acc_v, mix, home, own_exp, own_grad, early_score_grad, early_query, top, norm, delta,
+    local_sem, kv_send, kv_recv, pass_send, cnt_send, cnt_recv, swap_send, swap_recv,
+    back_send, back_recv,
 ):
     halo = n // 4
     me = lax.axis_index("seq")
@@ -67,28 +69,59 @@
         barrier, jnp.minimum(me, halo) + jnp.minimum(n - 1 - me, halo) + (ndp - 1)
     )
 
-    def halo_copies(j):
-        target = {"seq": me + j}
-        place = pl.ds((halo - j) * rows, rows)
-        return [
-            pltpu.make_async_remote_copy(
-                src, dst, kv_send.at[j - 1, i], kv_recv.at[j - 1, i],
-                device_id=target, device_id_type=MESH,
-            )
-            for i, (src, dst) in enumerate(
-                [
-                    (k_hbm, kbuf.at[place]),
-                    (v_hbm, vbuf.at[place]),
-                    (seg_ref, sbuf.at[halo - j]),
-                ]
-            )
-        ]
+    odd = lax.rem(me, 2) == 1
+
+    def when(*terms):
+        terms = [term for term in terms if term is not True]
+        if any(term is False for term in terms):
+            return lambda body: None
+        return pl.when(functools.reduce(jnp.logical_and, terms))
+
+    def block(j):
+        return pl.ds((halo - j) * rows, rows)
+
+    def crosses(j, later_odd):
+        later_even = jnp.logical_not(later_odd)
+        return (True if j == 1 else later_even, True if j == halo else later_odd)
+
+    def passes_on(j):
+        return (
+            jnp.logical_not(odd) if j < halo else False,
+            odd if j > 1 else False,
+        )
+
+    def kv_copy(i, j):
+        return pltpu.make_async_remote_copy(
+            (k_hbm, v_hbm)[i], (kbuf, vbuf)[i].at[block(j)],
+            kv_send.at[j - 1, i], kv_recv.at[j - 1, i],
+            device_id={"seq": me + j}, device_id_type=MESH,
+        )
+
+    def seg_copy(j):
+        return pltpu.make_async_remote_copy(
+            seg_ref, sbuf.at[halo - j], kv_send.at[j - 1, 2], kv_recv.at[j - 1, 2],
+            device_id={"seq": me + j}, device_id_type=MESH,
+        )
+
+    def pass_copy(i, j):
+        step = 1 - 2 * i
+        buf = (kbuf, vbuf)[i]
+        return pltpu.make_async_remote_copy(
+            buf.at[block(j)], buf.at[block(j + step)],
+            pass_send.at[j - 1, i], kv_recv.at[j + step - 1, i],
+            device_id={"seq": me + step}, device_id_type=MESH,
+        )
 
     for j in range(halo, 0, -1):
-        @pl.when(me + j < n)
-        def _():
-            for copy in halo_copies(j):
-                copy.start()
+        later_odd = lax.rem(me + j, 2) == 1
+        for i in range(2):
+            @when(me + j < n, crosses(j, later_odd)[i])
+            def _():
+                kv_copy(i, j).start()
+
+        @when(me + j < n)
+        def _():
+            seg_copy(j).start()
 
     cbuf[0] = jnp.full((8, 128), cnt_ref[0].astype(jnp.float32))
 
@@ -109,24 +142,9 @@
             vbuf[pl.ds((halo - j) * rows, rows), :] = jnp.zeros((rows, KV_WIDTH), jnp.bfloat16)
             sbuf[halo - j] = jnp.full((1, rows), -1, jnp.int32)
 
-    for load in loads:
-        load.wait()
-    for j in range(1, ndp):
-        count_copy(j).wait_recv()
-    for j in range(1, halo + 1):
-        @pl.when(me - j >= 0)
-        def _():
-            for copy in halo_copies(j):
-                copy.wait_recv()
-
-    total = cbuf[0]
-    for j in range(1, ndp):
-        total = total + cbuf[j]
-    factor = (float(ndp * n * rows) / total)[0:1, :]
-    scaled = factor * SCALE
-
     q_doc = seg_ref[...].astype(jnp.float32)
-    for b in range(halo + 1):
+
+    def prepare(b):
         k_doc = jnp.transpose(jnp.broadcast_to(sbuf[b].astype(jnp.float32), (rows, rows)))
         allowed = k_doc == q_doc
         if b == halo:
@@ -143,19 +161,31 @@
             ktslot[s, :, place] = jnp.transpose(tile)
             vslot[s, place, :] = vbuf[place, lanes]
 
-    def pair(p, carry):
+    def pair_cols(p):
+        return pl.ds(pl.multiple_of(p * 2 * HEAD_DIM, 2 * HEAD_DIM), 2 * HEAD_DIM)
+
+    def both_slots(buf, p, place):
+        first, second = slot_ref[2 * p], slot_ref[2 * p + 1]
+        return jnp.concatenate([buf[first, place, :], buf[second, place, :]], axis=1)
+
+    def accumulate(p, place, k_part, v_part):
         h1 = 2 * p
-        h2 = h1 + 1
-        s1, s2 = slot_ref[h1], slot_ref[h2]
+        s1, s2 = slot_ref[h1], slot_ref[h1 + 1]
         before = slot_ref[lax.rem(h1 + HEADS - 1, HEADS)]
         keep1 = jnp.where(before == s1, 1.0, 0.0)
         keep2 = jnp.where(s1 == s2, 1.0, 0.0)
-        cols = pl.ds(pl.multiple_of(p * 2 * HEAD_DIM, 2 * HEAD_DIM), 2 * HEAD_DIM)
+        for acc, part in ((acc_k, k_part), (acc_v, v_part)):
+            first = acc[h1, place, :] * keep1 + part[:, :HEAD_DIM]
+            acc[h1 + 1, place, :] = first
+            acc[h1 + 2, place, :] = first * keep2 + part[:, HEAD_DIM:]
+
+    own = pl.ds(halo * rows, rows)
+    early = pl.ds(0, halo * rows)
+
+    def own_scores(p):
+        cols = pair_cols(p)
         q2, g2, o2 = qbuf[:, cols], gbuf[:, cols], obuf[:, cols]
         q_diag, g_diag = block_diag(q2), block_diag(g2)
-        k_cat = jnp.concatenate([kslot[s1], kslot[s2]], axis=1)
-        v_cat = jnp.concatenate([vslot[s1], vslot[s2]], axis=1)
-
         product = g2.astype(jnp.float32) * o2.astype(jnp.float32)
         high = product.astype(jnp.bfloat16)
         low = (product - high.astype(jnp.float32)).astype(jnp.bfloat16)
@@ -167,63 +197,195 @@
             axis=0,
         )
         ones = jnp.ones((16, 2 * HEAD_DIM), jnp.bfloat16)
-        delta = dot(ones, terms, ((1,), (1,)))[0:1, :]
-
-        scores = dot(k_cat, q_diag, ((1,), (1,))) + bias[...]
-        top = jnp.max(scores, axis=0, keepdims=True)
-        expd = jnp.exp2((scores - top) * EXP2_SCALE)
-        weights = expd * (1.0 / jnp.sum(expd, axis=0, keepdims=True))
-        grad_weights = dot(v_cat, g_diag, ((1,), (1,)))
-        score_grad = (weights * (grad_weights - delta)).astype(jnp.bfloat16)
-
-        v_part = dot(weights.astype(jnp.bfloat16), g_diag, ((1,), (0,)))
-        k_part = dot(score_grad, q_diag, ((1,), (0,)))
-        for acc, part in ((acc_k, k_part), (acc_v, v_part)):
-            first = acc[h1] * keep1 + part[:, :HEAD_DIM]
-            acc[h1 + 1] = first
-            acc[h1 + 2] = first * keep2 + part[:, HEAD_DIM:]
-
+        row_delta = dot(ones, terms, ((1,), (1,)))[0:1, :]
+        scores = dot(both_slots(kslot, p, own), q_diag, ((1,), (1,))) + bias[own, :]
+        peak = jnp.max(scores, axis=0, keepdims=True)
+        expd = jnp.exp2((scores - peak) * EXP2_SCALE)
+        own_exp[p] = expd
+        own_grad[p] = dot(both_slots(vslot, p, own), g_diag, ((1,), (1,))) - row_delta
+        top[p] = peak
+        norm[p] = jnp.sum(expd, axis=0, keepdims=True)
+        delta[p] = row_delta
+
+    def early_grads(p):
+        cols = pair_cols(p)
+        q_diag, g_diag = block_diag(qbuf[:, cols]), block_diag(gbuf[:, cols])
+        scores = dot(both_slots(kslot, p, early), q_diag, ((1,), (1,))) + bias[early, :]
+        own_top = top[p]
+        peak = jnp.maximum(own_top, jnp.max(scores, axis=0, keepdims=True))
+        expd = jnp.exp2((scores - peak) * EXP2_SCALE)
+        shrink = jnp.exp2((own_top - peak) * EXP2_SCALE)
+        inverse = 1.0 / (jnp.sum(expd, axis=0, keepdims=True) + norm[p] * shrink)
+        norm[p] = shrink * inverse
+        weights = expd * inverse
+        grad_weights = dot(both_slots(vslot, p, early), g_diag, ((1,), (1,)))
+        score_grad = (weights * (grad_weights - delta[p])).astype(jnp.bfloat16)
+        if halo <= 2:
+            early_score_grad[p] = score_grad
+        else:
+            for i in range(2):
+                kt = ktslot[slot_ref[2 * p + i], :, early]
+                early_query[p, i] = dot(kt, score_grad[:, i * HEAD_DIM:(i + 1) * HEAD_DIM], ((1,), (0,)))
+        accumulate(
+            p, early,
+            dot(score_grad, q_diag, ((1,), (0,))),
+            dot(weights.astype(jnp.bfloat16), g_diag, ((1,), (0,))),
+        )
+
+    def own_grads(p):
+        cols = pair_cols(p)
+        q_diag, g_diag = block_diag(qbuf[:, cols]), block_diag(gbuf[:, cols])
+        weights = own_exp[p] * norm[p]
+        score_grad = (weights * own_grad[p]).astype(jnp.bfloat16)
+        accumulate(
+            p, own,
+            dot(score_grad, q_diag, ((1,), (0,))),
+            dot(weights.astype(jnp.bfloat16), g_diag, ((1,), (0,))),
+        )
         turned = []
-        for i, s in enumerate((s1, s2)):
-            dqt = dot(ktslot[s], score_grad[:, i * HEAD_DIM:(i + 1) * HEAD_DIM], ((1,), (0,)))
+        for i in range(2):
+            lanes = slice(i * HEAD_DIM, (i + 1) * HEAD_DIM)
+            slot = slot_ref[2 * p + i]
+            if halo <= 2:
+                every = jnp.concatenate([early_score_grad[p], score_grad], axis=0)
+                dqt = dot(ktslot[slot], every[:, lanes], ((1,), (0,)))
+            else:
+                dqt = early_query[p, i] + dot(ktslot[slot, :, own], score_grad[:, lanes], ((1,), (0,)))
             turned.append((jnp.transpose(dqt) * scaled).astype(jnp.bfloat16))
-        dq_ref[:, cols] = jnp.concatenate(turned, axis=1)
-        return carry
+        qbuf[:, cols] = jnp.concatenate(turned, axis=1)
+
+    def all_pairs(step, first=0, last=4):
+        unroll = UNROLL if halo <= 2 else 1
+
+        def body(i, carry):
+            for u in range(unroll):
+                step(i * unroll + u)
+            return carry
+
+        quarter = HEADS // 8 // unroll
+        lax.fori_loop(first * quarter, last * quarter, body, 0)
 
     acc_k[0] = jnp.zeros(acc_k.shape[1:], jnp.float32)
     acc_v[0] = jnp.zeros(acc_v.shape[1:], jnp.float32)
-    lax.fori_loop(0, HEADS // 2, pair, 0)
+    for load in loads:
+        load.wait()
+    prepare(halo)
+    all_pairs(own_scores)
+
+    for j in range(1, ndp):
+        count_copy(j).wait_recv()
+    total = cbuf[0]
+    for j in range(1, ndp):
+        total = total + cbuf[j]
+    factor = (float(ndp * n * rows) / total)[0:1, :]
+    scaled = factor * SCALE
+
+    for j in range(1, halo + 1):
+        for i in range(2):
+            @when(me - j >= 0, passes_on(j)[i])
+            def _():
+                kv_copy(i, j).wait_recv()
+                pass_copy(i, j).start()
+
+    for j in range(1, halo + 1):
+        @when(me - j >= 0)
+        def _():
+            seg_copy(j).wait_recv()
+
+        for i in range(2):
+            @when(me - j >= 0, True if passes_on(j)[i] is False else jnp.logical_not(passes_on(j)[i]))
+            def _():
+                kv_copy(i, j).wait_recv()
+
+        prepare(halo - j)
+    all_pairs(early_grads)
 
     lasts = [jnp.int32(0)] * KV_SLOTS
     for h in range(HEADS):
         slot = slot_ref[h]
         lasts = [last + (slot <= s).astype(jnp.int32) for s, last in enumerate(lasts)]
 
-    def back_copy(j):
-        return pltpu.make_async_remote_copy(
-            back.at[j - 1], home.at[j - 1], back_send.at[j - 1], back_recv.at[j - 1],
+    def part(i, j, s):
+        return (acc_k, acc_v)[i][lasts[s], block(j), :] * (scaled, factor)[i]
+
+    def back_copy(i, j):
+        return pltpu.make_async_remote_copy(
+            (kbuf, vbuf)[i].at[block(j)], home.at[j - 1, i],
+            back_send.at[j - 1, i], back_recv.at[j - 1, i],
             device_id={"seq": me - j}, device_id_type=MESH,
         )
 
-    for j in range(halo, 0, -1):
-        place = pl.ds((halo - j) * rows, rows)
+    def swap_copy(i, j):
+        place = j - 2 if i == 0 else j - 1
+        return pltpu.make_async_remote_copy(
+            (kbuf, vbuf)[i].at[block(j)], mix.at[place], swap_send.at[place], swap_recv.at[place],
+            device_id={"seq": me - 1 if i == 0 else me + 1}, device_id_type=MESH,
+        )
+
+    def stage(i, j, place=None):
         for s in range(KV_SLOTS):
             lanes = pl.ds(s * HEAD_DIM, HEAD_DIM)
-            back[j - 1, 0, :, lanes] = (acc_k[lasts[s], place, :] * scaled).astype(jnp.bfloat16)
-            back[j - 1, 1, :, lanes] = (acc_v[lasts[s], place, :] * factor).astype(jnp.bfloat16)
-
-        @pl.when(me - j >= 0)
-        def _():
-            back_copy(j).start()
-
-    for j in range(1, halo + 1):
-        @pl.when(me + j >= n)
-        def _():
-            home[j - 1] = jnp.zeros(home.shape[1:], jnp.bfloat16)
-
-        @pl.when(me + j < n)
-        def _():
-            back_copy(j).wait_recv()
+            value = part(i, j, s)
+            if place is not None:
+                value = value + mix[place, :, lanes].astype(jnp.float32)
+            (kbuf, vbuf)[i][block(j), lanes] = value.astype(jnp.bfloat16)
+
+    even = jnp.logical_not(odd)
+    for j in range(1, halo + 1):
+        for i in range(2):
+            @when(me - j >= 0, passes_on(j)[i])
+            def _():
+                pass_copy(i, j).wait_send()
+
+    for j in range(1, halo + 1):
+        @when(me - j >= 0, even, j < halo)
+        def _():
+            stage(1, j)
+            swap_copy(1, j).start()
+
+        @when(me - j >= 0, odd, j > 1)
+        def _():
+            stage(0, j)
+            swap_copy(0, j).start()
+
+    for j, mine in ((halo, even), (1, odd)):
+        @when(me - j >= 0, mine)
+        def _():
+            for i in range(2):
+                stage(i, j)
+                back_copy(i, j).start()
+
+    all_pairs(own_grads, 0, 1)
+
+    for j in range(1, halo + 1):
+        @when(me - j >= 0, even, j < halo)
+        def _():
+            swap_copy(0, j + 1).wait_recv()
+            stage(0, j, j - 1)
+            back_copy(0, j).start()
+
+        @when(me - j >= 0, odd, j > 1)
+        def _():
+            swap_copy(1, j - 1).wait_recv()
+            stage(1, j, j - 2)
+            back_copy(1, j).start()
+
+    all_pairs(own_grads, 1, 4)
+    store_dq = pltpu.make_async_copy(qbuf, dq_hbm, local_sem.at[2])
+    store_dq.start()
+
+    for j in range(1, halo + 1):
+        later_odd = lax.rem(me + j, 2) == 1
+        for i in range(2):
+            sent = crosses(j, later_odd)[i]
+
+            @when(me + j < n, sent)
+            def _():
+                back_copy(i, j).wait_recv()
+
+            @pl.when(jnp.logical_not(jnp.logical_and(me + j < n, sent)))
+            def _():
+                home[j - 1, i] = jnp.zeros(home.shape[2:], jnp.bfloat16)
 
     place = pl.ds(halo * rows, rows)
     for s in range(KV_SLOTS):
@@ -234,17 +396,32 @@
                 value = value + home[j, i, :, lanes].astype(jnp.float32)
             out[:, lanes] = value.astype(jnp.bfloat16)
 
+    store_dq.wait()
     for j in range(1, ndp):
         count_copy(j).wait_send()
     for j in range(1, halo + 1):
-        @pl.when(me + j < n)
-        def _():
-            for copy in halo_copies(j):
-                copy.wait_send()
-
-        @pl.when(me - j >= 0)
-        def _():
-            back_copy(j).wait_send()
+        later_odd = lax.rem(me + j, 2) == 1
+
+        @when(me + j < n)
+        def _():
+            seg_copy(j).wait_send()
+
+        for i in range(2):
+            @when(me + j < n, crosses(j, later_odd)[i])
+            def _():
+                kv_copy(i, j).wait_send()
+
+            @when(me - j >= 0, crosses(j, odd)[i])
+            def _():
+                back_copy(i, j).wait_send()
+
+        @when(me - j >= 0, even, j < halo)
+        def _():
+            swap_copy(1, j).wait_send()
+
+        @when(me - j >= 0, odd, j > 1)
+        def _():
+            swap_copy(0, j).wait_send()
 
 
 def local(queries, keys, values, attn_out, out_grad, segments, token_counts, head_slot):
@@ -265,7 +442,7 @@
             jax.ShapeDtypeStruct((rows, KV_WIDTH), bf16),
         ],
         in_specs=[hbm] * 5 + [vmem, smem, smem],
-        out_specs=[vmem] * 3,
+        out_specs=[hbm, vmem, vmem],
         scratch_shapes=[
             pltpu.VMEM((rows, WIDTH), bf16),
             pltpu.VMEM((rows, WIDTH), bf16),
@@ -280,15 +457,25 @@
             pltpu.VMEM((span, 2 * HEAD_DIM), f32),
             pltpu.VMEM((HEADS + 1, span, HEAD_DIM), f32),
             pltpu.VMEM((HEADS + 1, span, HEAD_DIM), f32),
+            pltpu.VMEM((halo - 1, rows, KV_WIDTH), bf16),
             pltpu.VMEM((halo, 2, rows, KV_WIDTH), bf16),
-            pltpu.VMEM((halo, 2, rows, KV_WIDTH), bf16),
+            pltpu.VMEM((HEADS // 2, rows, 2 * HEAD_DIM), f32),
+            pltpu.VMEM((HEADS // 2, rows, 2 * HEAD_DIM), f32),
+            pltpu.VMEM((HEADS // 2 if halo <= 2 else 1, halo * rows, 2 * HEAD_DIM), bf16),
+            pltpu.VMEM((1 if halo <= 2 else HEADS // 2, 2, HEAD_DIM, rows), f32),
+            pltpu.VMEM((HEADS // 2, 1, 2 * HEAD_DIM), f32),
+            pltpu.VMEM((HEADS // 2, 1, 2 * HEAD_DIM), f32),
+            pltpu.VMEM((HEADS // 2, 1, 2 * HEAD_DIM), f32),
             dma((5,)),
             dma((halo, 3)),
             dma((halo, 3)),
+            dma((halo, 2)),
             dma((ndp,)),
             dma((ndp,)),
-            dma((halo,)),
-            dma((halo,)),
+            dma((halo - 1,)),
+            dma((halo - 1,)),
+            dma((halo, 2)),
+            dma((halo, 2)),
         ],
         compiler_params=pltpu.CompilerParams(
             collective_id=0, has_side_effects=True, vmem_limit_bytes=60 * 1024 * 1024

time: 44.3 us -> 34.9 us (0.79)
  Pallas kernels: 38.9 us -> 29.5 us
    pallas_call x1, Pallas kernels: 38.9 us -> 29.5 us  [local(): pl.pallas_call(functools.partial(kernel, n, ndp, rows), out_shape=[jax.Sh...]
where the time goes in v2:
time: 34.9 us; the launch traced here: 34.7 us
  Pallas kernels  29.5 us (85%)
  local copies, waits for them, and re-layouts  3.93 us (11%)
  between operations  1.3 us (4%)
    pallas_call x1, Pallas kernels, local(): pl.pallas_call(functools.partial(kernel, n, ndp, rows), out_shape=[jax.Sh...  29.5 us
    unnamed x7, local copies, waits for them, and re-layouts  3.93 us

profile of v2, /device:TPU:3, one launch (start us, length us, event | category | flops | bytes accessed | tf_op | source)
XLA Modules:
  0.0 34.7 jit_solution(2312454841899353783)
XLA Ops:
  1.3 29.5 %shard_map.103 = (bf16[128,4096]{1,0:T(8,128)(2,1)}, bf16[128,512]{1,0:T(8,128)(2,1)}, bf16[128,512]{1,0:T(8,128)(2,1)}) custom-call(bf16[128,4096]{1,0:T(8,128)(2,1)} %bitcast.9, bf16[128,512]{1,0:T(8,128)(2,1)} %bitcast.14, bf16[128,512]{1,0:T(8,128)(2,1)} %bitcast.15, bf16[128,4096]{1,0:T(8,128)(2,1)} %bitcast.10, bf16[128,4096]{1,0:T(8,128)(2,1)} %bitcast.11, ...), custom_call_target="tpu_custom_call" | custom-call | tf_op jit(solution)/shard_map/pallas_call | solution.py:437
  30.8 0.0 copy-start.1
  30.8 2.3 %copy.15 = bf16[1,128,4096]{2,1,0:T(8,128)(2,1)} copy(bf16[1,128,4096]{2,1,0:T(8,128)(2,1)} %bitcast.8) | data formatting | bytes 2097152
  33.1 0.0 copy-done.1
  33.1 0.0 copy-start
  33.1 0.7 %copy.16 = bf16[1,128,512]{2,1,0:T(8,128)(2,1)} copy(bf16[1,128,512]{2,1,0:T(8,128)(2,1)S(1)} %bitcast.13) | data formatting | bytes 262144
  33.8 0.3 copy-done
  34.1 0.7 %copy.17 = bf16[1,128,512]{2,1,0:T(8,128)(2,1)} copy(bf16[1,128,512]{2,1,0:T(8,128)(2,1)S(1)} %bitcast.12) | data formatting | bytes 262144
Async XLA Ops:
  30.8 2.3 %copy-start.1 = (bf16[128,512]{1,0:T(8,128)(2,1)S(1)}, bf16[128,512]{1,0:T(8,128)(2,1)}, u32[]{:S(2)}) copy-start(bf16[128,512]{1,0:T(8,128)(2,1)} %get-tuple-element.7) | copy-start | bytes 393220
  33.1 1.0 %copy-start = (bf16[128,512]{1,0:T(8,128)(2,1)S(1)}, bf16[128,512]{1,0:T(8,128)(2,1)}, u32[]{:S(2)}) copy-start(bf16[128,512]{1,0:T(8,128)(2,1)} %get-tuple-element.8) | copy-start | bytes 393220

commit v3 on v2

--- a/solution.py
+++ b/solution.py
@@ -156,10 +156,13 @@
         bias[place, :] = jnp.concatenate([one, one], axis=1)
         for s in range(KV_SLOTS):
             lanes = pl.ds(s * HEAD_DIM, HEAD_DIM)
-            tile = kbuf[place, lanes]
-            kslot[s, place, :] = tile
-            ktslot[s, :, place] = jnp.transpose(tile)
+            kslot[s, place, :] = kbuf[place, lanes]
             vslot[s, place, :] = vbuf[place, lanes]
+
+    def turn_keys(b):
+        place = pl.ds(b * rows, rows)
+        for s in range(KV_SLOTS):
+            ktslot[s, :, place] = jnp.transpose(kslot[s, place, :])
 
     def pair_cols(p):
         return pl.ds(pl.multiple_of(p * 2 * HEAD_DIM, 2 * HEAD_DIM), 2 * HEAD_DIM)
@@ -269,7 +272,13 @@
     acc_v[0] = jnp.zeros(acc_v.shape[1:], jnp.float32)
     for load in loads:
         load.wait()
+    lasts = [jnp.int32(0)] * KV_SLOTS
+    for h in range(HEADS):
+        slot = slot_ref[h]
+        lasts = [last + (slot <= s).astype(jnp.int32) for s, last in enumerate(lasts)]
+
     prepare(halo)
+    turn_keys(halo)
     all_pairs(own_scores)
 
     for j in range(1, ndp):
@@ -298,12 +307,9 @@
                 kv_copy(i, j).wait_recv()
 
         prepare(halo - j)
+        if halo > 2:
+            turn_keys(halo - j)
     all_pairs(early_grads)
-
-    lasts = [jnp.int32(0)] * KV_SLOTS
-    for h in range(HEADS):
-        slot = slot_ref[h]
-        lasts = [last + (slot <= s).astype(jnp.int32) for s, last in enumerate(lasts)]
 
     def part(i, j, s):
         return (acc_k, acc_v)[i][lasts[s], block(j), :] * (scaled, factor)[i]
@@ -355,6 +361,9 @@
                 stage(i, j)
                 back_copy(i, j).start()
 
+    if halo <= 2:
+        for j in range(1, halo + 1):
+            turn_keys(halo - j)
     all_pairs(own_grads, 0, 1)
 
     for j in range(1, halo + 1):
@@ -422,6 +431,28 @@
         @when(me - j >= 0, odd, j > 1)
         def _():
             swap_copy(0, j).wait_send()
+
+
+PIECES = 4
+
+
+def settle(dq_in, dk_in, dv_in, dq_out, dk_out, dv_out, dq_held, dk_held, dv_held, sems):
+    rows = dq_in.shape[0] // PIECES
+    moves = []
+    for i in range(PIECES):
+        place = pl.ds(i * rows, rows)
+        moves.append((dq_in.at[place], dq_held.at[place], dq_out.at[place]))
+    moves.append((dk_in, dk_held, dk_out))
+    moves.append((dv_in, dv_held, dv_out))
+    reads = [pltpu.make_async_copy(m[0], m[1], sems.at[0, i]) for i, m in enumerate(moves)]
+    writes = [pltpu.make_async_copy(m[1], m[2], sems.at[1, i]) for i, m in enumerate(moves)]
+    for read in reads:
+        read.start()
+    for read, write in zip(reads, writes):
+        read.wait()
+        write.start()
+    for write in writes:
+        write.wait()
 
 
 def local(queries, keys, values, attn_out, out_grad, segments, token_counts, head_slot):
@@ -481,6 +512,13 @@
             collective_id=0, has_side_effects=True, vmem_limit_bytes=60 * 1024 * 1024
         ),
     )(queries[0], keys[0], values[0], attn_out[0], out_grad[0], segments, token_counts, head_slot)
+    dq, dk, dv = pl.pallas_call(
+        settle,
+        out_shape=[jax.ShapeDtypeStruct(x.shape, bf16) for x in (dq, dk, dv)],
+        in_specs=[hbm] * 3,
+        out_specs=[hbm] * 3,
+        scratch_shapes=[pltpu.VMEM(x.shape, bf16) for x in (dq, dk, dv)] + [dma((2, PIECES + 2))],
+    )(dq, dk, dv)
     return dq[None], dk[None], dv[None]
 
 

time: 34.9 us -> 32.9 us (0.943)
  local copies, waits for them, and re-layouts: 3.93 us -> 0 us
  Pallas kernels: 29.5 us -> 31.4 us
    unnamed x7 -> x0, local copies, waits for them, and re-layouts: 3.93 us -> none
    pallas_call x0 -> x1, Pallas kernels: none -> 2.1 us  [local(): pl.pallas_call(settle, out_shape=[jax.ShapeDtypeStruct(x.shape, bf16) for...]
where the time goes in v3:
time: 32.9 us; the launch traced here: 32.7 us
  Pallas kernels  31.4 us (95%)
  between operations  1.29 us (4%)
    pallas_call x1, Pallas kernels, local(): pl.pallas_call(functools.partial(kernel, n, ndp, rows), out_shape=[jax.Sh...  29.3 us
    pallas_call x1, Pallas kernels, local(): pl.pallas_call(settle, out_shape=[jax.ShapeDtypeStruct(x.shape, bf16) for...  2.1 us

profile of v3, /device:TPU:3, one launch (start us, length us, event | category | flops | bytes accessed | tf_op | source)
XLA Modules:
  0.0 32.7 jit_solution(435682781302363768)
XLA Ops:
  1.3 29.3 %shard_map.103 = (bf16[128,4096]{1,0:T(8,128)(2,1)}, bf16[128,512]{1,0:T(8,128)(2,1)}, bf16[128,512]{1,0:T(8,128)(2,1)}) custom-call(bf16[128,4096]{1,0:T(8,128)(2,1)} %bitcast.8, bf16[128,512]{1,0:T(8,128)(2,1)} %bitcast.11, bf16[128,512]{1,0:T(8,128)(2,1)} %bitcast.12, bf16[128,4096]{1,0:T(8,128)(2,1)} %bitcast.9, bf16[128,4096]{1,0:T(8,128)(2,1)} %bitcast.10, ...), custom_call_target="tpu_custom_call" | custom-call | tf_op jit(solution)/shard_map/pallas_call | solution.py:468
  30.6 2.1 %shard_map.104 = (bf16[128,4096]{1,0:T(8,128)(2,1)}, bf16[128,512]{1,0:T(8,128)(2,1)}, bf16[128,512]{1,0:T(8,128)(2,1)}) custom-call(bf16[128,4096]{1,0:T(8,128)(2,1)} %get-tuple-element.9.dq_in, bf16[128,512]{1,0:T(8,128)(2,1)} %get-tuple-element.10.dk_in, bf16[128,512]{1,0:T(8,128)(2,1)} %get-tuple-element.11.dv_in), custom_call_target="tpu_custom_call" | custom-call | tf_op jit(solution)/shard_map/pallas_call | solution.py:515
